TPU v7x, 512 devices: a whole 4x4x16 slice. The times are simulated.
512 devices in a mesh: section: 8 (over x, core), mp: 64 (over y, z).
Axes of the slice: x: 4, y: 4, z: 16, core: 2. Of those that a mesh axis runs over, the one named last changes fastest.
Arguments:
- section_in: bfloat16 [8, 128, 8192], P('section', 'mp'), may hold values from -8 to 8
- fresh: bfloat16 [128, 8192], P('mp'), may hold values from -8 to 8
- latents: bfloat16 [72, 64, 1280], P(None, 'mp'), may hold values from -4 to 4
- image_order: int32 [72], replicated, may hold values from 0 to 71, each once
- token_mask: int32 [9, 128, 8], replicated, may hold values from 0 to 1, as said below
- norm_gain: bfloat16 [8, 8192], P('section'), may hold values from 0.5 to 1.5
- wq: bfloat16 [8, 8192, 8192], P('section', None, 'mp'), may hold values from -0.1875 to 0.1875
- wkv: bfloat16 [8, 2, 1280, 8192], P('section', None, None, 'mp'), may hold values from -3 to 3
- wo: bfloat16 [8, 8192, 8192], P('section', None, 'mp'), may hold values from -0.1875 to 0.1875
- alpha: float32 [8, 8192], P('section', 'mp'), may hold values from 0.5 to 1.5
Outputs:
- first_out: bfloat16 [8, 128, 8192], P('section', 'mp')
- second_out: bfloat16 [8, 128, 8192], P('section', 'mp')
Inputs may be any that keep to these rules, and one draw needn't show every extreme that they name: `image_order`: each image index once. `token_mask`: in every micro-batch the first 8 tokens, and possibly more, see no slot.
All inputs are finite; a program needn't handle non-finite values.
Results may differ from a plain program's by a relative error of at most 0.012.
The roundings to bfloat16 on the way count: a program that leaves them out, or rounds other values in their place, can miss the bound.
Values may be sent and summed in bfloat16 or wider, within the bound.
A program may use at most 64 MiB of HBM per device.

v0:
```python
import jax
import jax.numpy as jnp
from jax import lax
from jax.sharding import PartitionSpec as P

HD = 128
LAT = 64
IMG_MB = 8


epsilon = 1e-05
negative_big = -1e30


def from_behind(block, axis, distance):
    devices = range(lax.axis_size(axis))
    route = [(i - distance, i) for i in devices if i - distance in devices]
    return lax.ppermute(block, axis, route)


def rms_rows(hidden, norm_row):
    hidden32 = hidden.astype(jnp.float32)
    square_mean = jnp.mean(hidden32 * hidden32, axis=-1, keepdims=True)
    return (hidden32 * lax.rsqrt(square_mean + epsilon) * norm_row.astype(jnp.float32)).astype(
        jnp.bfloat16
    )


def attend(queries, key_rows, values, slot_mask):
    token_count = queries.shape[0]
    query_heads = queries.reshape(token_count, -1, HD)
    key_heads = key_rows.reshape(key_rows.shape[0], -1, HD)
    value_heads = values.reshape(values.shape[0], -1, HD)
    scores = jnp.einsum(
        "thd,lhd->htl", query_heads, key_heads, preferred_element_type=jnp.float32
    ) * HD ** (-0.5)
    visible = (jnp.repeat(slot_mask, LAT, axis=1) > 0)[None]
    seen_any = (jnp.sum(slot_mask, axis=1) > 0)[None, :, None]
    largest = jnp.max(jnp.where(visible, scores, negative_big), axis=-1, keepdims=True)
    largest = jnp.where(seen_any, largest, 0.0)
    expanded = jnp.where(visible, jnp.exp(jnp.where(visible, scores - largest, 0.0)), 0.0)
    totals = jnp.sum(expanded, axis=-1, keepdims=True)
    totals = jnp.where(seen_any, totals, 1.0)
    probs = (expanded / totals).astype(jnp.bfloat16)
    mixed = jnp.einsum("htl,lhd->thd", probs, value_heads, preferred_element_type=jnp.float32)
    return mixed.reshape(token_count, -1)


def local(section_in, fresh, latents, image_order, token_mask, norm_gain, wq, wkv, wo, alpha):
    section_count = lax.axis_size("section")
    section_index = lax.axis_index("section")
    norm_row = norm_gain[0]
    proj_query = wq[0]
    proj_latent = jnp.concatenate([wkv[0, 0], wkv[0, 1]], axis=1)
    proj_out = wo[0]
    head_width = proj_query.shape[1]
    scale_row = jnp.tanh(alpha[0])

    def project(part_rows):
        flattened = part_rows.reshape(-1, part_rows.shape[2])
        made = jnp.dot(flattened, proj_latent, preferred_element_type=jnp.float32).astype(
            jnp.bfloat16
        )
        return made.reshape(part_rows.shape[0], part_rows.shape[1], -1)

    def chosen(micro):
        image_ids = lax.dynamic_slice_in_dim(image_order, micro * IMG_MB, IMG_MB)
        return jnp.take(latents, image_ids, axis=0)

    def fetch(micro):
        return project(lax.all_gather(chosen(micro), "mp", axis=1, tiled=True))

    first_micro = section_count - 1 - section_index
    second_micro = section_count - section_index
    first_keys = fetch(first_micro)
    second_keys = fetch(second_micro)
    first_mask = lax.dynamic_index_in_dim(token_mask, first_micro, 0, keepdims=False)
    second_mask = lax.dynamic_index_in_dim(token_mask, second_micro, 0, keepdims=False)

    def add_heads(piece):
        return jnp.dot(piece, proj_out, preferred_element_type=jnp.float32)

    def branch(queries, key_values, slot_mask):
        flattened = key_values.reshape(-1, key_values.shape[2])
        attended = attend(
            queries, flattened[:, :head_width], flattened[:, head_width:], slot_mask
        ).astype(jnp.bfloat16)
        projected = add_heads(lax.all_gather(attended, "mp", axis=1, tiled=True))
        return (projected * scale_row[None, :]).astype(jnp.bfloat16)

    def query_part(part_rows):
        return jnp.dot(part_rows, proj_query, preferred_element_type=jnp.float32).astype(
            jnp.bfloat16
        )

    def advance(tok_rows, key_values, slot_mask):
        normed = rms_rows(tok_rows, norm_row)
        queries = query_part(lax.all_gather(normed, "mp", axis=0, tiled=True))
        returned = lax.all_to_all(
            branch(queries, key_values, slot_mask), "mp", split_axis=0, concat_axis=1, tiled=True
        )
        return (tok_rows.astype(jnp.float32) + returned.astype(jnp.float32)).astype(jnp.bfloat16)

    first_out = advance(section_in[0], first_keys, first_mask)
    shifted = from_behind(first_out, "section", 1)
    second_out = advance(jnp.where(section_index == 0, fresh, shifted), second_keys, second_mask)
    return (first_out[None], second_out[None])


def solution(mesh):
    in_specs = (
        P("section", "mp", None),
        P("mp", None),
        P(None, "mp", None),
        P(),
        P(),
        P("section", None),
        P("section", None, "mp"),
        P("section", None, None, "mp"),
        P("section", None, "mp"),
        P("section", "mp"),
    )
    out_specs = (P("section", "mp", None), P("section", "mp", None))
    return jax.shard_map(local, mesh=mesh, in_specs=in_specs, out_specs=out_specs, check_vma=False)
```

profile of v0, /device:TPU:6, one launch (start us, length us, event | category | flops | bytes accessed | tf_op | source)
XLA Modules:
  0.0 921.5 jit_solution(15773558459390610087)
XLA Ops:
  7.2 0.9 compare_and_fusion
  8.1 1.5 gather_fusion
  10.4 0.8 mul.90
  11.2 0.9 fusion.51
  12.2 1.5 fusion.62
  13.7 0.7 compare_bitcast_fusion
  14.6 0.7 dynamic-slice_reduce_fusion
  15.3 1.1 slice_bitcast_fusion.1
  16.5 139.3 %all-gather.11.cloned.1.call-done = bf16[8,64,1280]{2,0,1:T(8,128)(2,1)} async-done(((bf16[8,1,1280]{2,0,1:T(8,128)(2,1)}), bf16[8,64,1280]{2,0,1:T(8,128)(2,1)}) %all-gather.11.cloned.1.call-update) | async-done | bytes 1310736 | tf_op jit(solution)/shard_map/all_gather | solution.py:71
  155.8 1.5 copy.22
  157.3 1.2 convolution_convert_fusion.1
  158.6 137.6 %all-gather.19.cloned.1.call-done = bf16[64,2,8192]{2,1,0:T(2,128)(2,1)} async-done(((bf16[1,2,8192]{2,1,0:T(2,128)(2,1)}), bf16[64,2,8192]{2,1,0:T(2,128)(2,1)}) %all-gather.19.cloned.1.call-update) | async-done | bytes 2097168 | tf_op jit(solution)/shard_map/all_gather | solution.py:98
  296.2 4.1 reshape.216
  300.3 2.5 select_reduce_fusion.1
  303.1 1.8 fusion.36
  305.6 136.5 %all-gather.15.cloned.1.call-done = bf16[128,1,8192]{0,2,1:T(8,128)(2,1)} async-done(((bf16[128,1,128]{0,2,1:T(8,128)(2,1)}), bf16[128,1,8192]{0,2,1:T(8,128)(2,1)}) %all-gather.15.cloned.1.call-update) | async-done | bytes 2097168 | tf_op jit(solution)/shard_map/all_gather | solution.py:88
  442.1 3.6 fusion.25
  445.6 10.3 %all-to-all-start = ((bf16[64,2,128]{2,1,0:T(2,128)(2,1)}), bf16[64,2,128]{2,1,0:T(2,128)(2,1)S(1)}, u32[]{:S(2)}, u32[]{:S(2)}) async-start(bf16[64,2,128]{2,1,0:T(2,128)(2,1)} %bitcast.16), calls=%async_computation | async-start | bytes 65536 | tf_op jit(solution)/shard_map/all_to_all | solution.py:99
  456.7 13.6 %all-to-all-done = bf16[64,2,128]{2,1,0:T(2,128)(2,1)S(1)} async-done(((bf16[64,2,128]{2,1,0:T(2,128)(2,1)}), bf16[64,2,128]{2,1,0:T(2,128)(2,1)S(1)}, u32[]{:S(2)}, u32[]{:S(2)}) %all-to-all-start) | async-done | bytes 32800 | tf_op jit(solution)/shard_map/all_to_all | solution.py:99
  470.3 1.9 collective-permute-start
  472.3 3.3 collective-permute-done
  475.7 0.7 fusion.61
  476.7 123.9 %all-gather.13.cloned.1.call-done = bf16[8,64,1280]{2,0,1:T(8,128)(2,1)} async-done(((bf16[8,1,1280]{2,0,1:T(8,128)(2,1)}), bf16[8,64,1280]{2,0,1:T(8,128)(2,1)}) %all-gather.13.cloned.1.call-update) | async-done | bytes 1310736 | tf_op jit(solution)/shard_map/all_gather | solution.py:71
  600.7 1.5 copy.26
  602.7 138.1 %all-gather.21.cloned.1.call-done = bf16[64,2,8192]{2,1,0:T(2,128)(2,1)} async-done(((bf16[1,2,8192]{2,1,0:T(2,128)(2,1)}), bf16[64,2,8192]{2,1,0:T(2,128)(2,1)}) %all-gather.21.cloned.1.call-update) | async-done | bytes 2097168 | tf_op jit(solution)/shard_map/all_gather | solution.py:98
  740.9 4.1 reshape.218
  745.0 2.5 select_reduce_fusion
  747.7 0.9 fusion.37
  748.7 137.1 %all-gather.17.cloned.1.call-done = bf16[128,1,8192]{0,2,1:T(8,128)(2,1)} async-done(((bf16[128,1,128]{0,2,1:T(8,128)(2,1)}), bf16[128,1,8192]{0,2,1:T(8,128)(2,1)}) %all-gather.17.cloned.1.call-update) | async-done | bytes 2097168 | tf_op jit(solution)/shard_map/all_gather | solution.py:88
  885.8 3.6 fusion.20
  889.4 10.3 %all-to-all-start.1 = ((bf16[64,2,128]{2,1,0:T(2,128)(2,1)}), bf16[64,2,128]{2,1,0:T(2,128)(2,1)S(1)}, u32[]{:S(2)}, u32[]{:S(2)}) async-start(bf16[64,2,128]{2,1,0:T(2,128)(2,1)} %bitcast.29), calls=%async_computation.1 | async-start | bytes 65536 | tf_op jit(solution)/shard_map/all_to_all | solution.py:99
  900.3 13.7 %all-to-all-done.1 = bf16[64,2,128]{2,1,0:T(2,128)(2,1)S(1)} async-done(((bf16[64,2,128]{2,1,0:T(2,128)(2,1)}), bf16[64,2,128]{2,1,0:T(2,128)(2,1)S(1)}, u32[]{:S(2)}, u32[]{:S(2)}) %all-to-all-start.1) | async-done | bytes 32800 | tf_op jit(solution)/shard_map/all_to_all | solution.py:99
  (45 shorter events, 5.2 us)
Async XLA Ops:
  7.2 293.1 %copy-start = (bf16[1,8192,128]{2,1,0:T(8,128)(2,1)S(1)}, bf16[1,8192,128]{2,1,0:T(8,128)(2,1)}, u32[]{:S(2)}) copy-start(bf16[1,8192,128]{2,1,0:T(8,128)(2,1)} %param.18) | copy-start | bytes 6291460
  7.2 148.6 %all-gather.11.cloned.1.call-start = ((), (), s32[]{:S(2)}) async-start(), calls=%async_computation.2 | async-start | bytes 1331200 | tf_op jit(solution)/shard_map/all_gather | solution.py:71
  10.4 285.8 %all-gather.19.cloned.1.call-start = ((), (), s32[]{:S(2)}) async-start(), calls=%async_computation.6 | async-start | bytes 2129920 | tf_op jit(solution)/shard_map/all_gather | solution.py:98
  13.7 428.4 %all-gather.15.cloned.1.call-start = ((), (), s32[]{:S(2)}) async-start(), calls=%async_computation.4 | async-start | bytes 2129920 | tf_op jit(solution)/shard_map/all_gather | solution.py:88
  300.3 4.7 copy-start.1
  300.3 5.3 copy-start.4
  305.5 164.7 %copy-start.2 = (bf16[1,2,8192]{2,1,0:T(2,128)(2,1)S(1)}, bf16[1,2,8192]{2,1,0:T(2,128)(2,1)}, u32[]{:S(2)}) copy-start(bf16[1,2,8192]{2,1,0:T(2,128)(2,1)} %param.12) | copy-start | bytes 98308
  305.6 170.0 %copy-start.3 = (bf16[2,8192]{1,0:T(2,128)(2,1)S(1)}, bf16[2,8192]{1,0:T(2,128)(2,1)}, u32[]{:S(2)}) copy-start(bf16[2,8192]{1,0:T(2,128)(2,1)} %param.13) | copy-start | bytes 98308
  445.6 24.6 %all-to-all-start = ((bf16[64,2,128]{2,1,0:T(2,128)(2,1)}), bf16[64,2,128]{2,1,0:T(2,128)(2,1)S(1)}, u32[]{:S(2)}, u32[]{:S(2)}) async-start(bf16[64,2,128]{2,1,0:T(2,128)(2,1)} %bitcast.16), calls=%async_computation | async-start | bytes 65536 | tf_op jit(solution)/shard_map/all_to_all | solution.py:99
  455.9 144.7 %all-gather.13.cloned.1.call-start = ((), (), s32[]{:S(2)}) async-start(), calls=%async_computation.3 | async-start | bytes 1331200 | tf_op jit(solution)/shard_map/all_gather | solution.py:71
  456.7 284.2 %all-gather.21.cloned.1.call-start = ((), (), s32[]{:S(2)}) async-start(), calls=%async_computation.7 | async-start | bytes 2129920 | tf_op jit(solution)/shard_map/all_gather | solution.py:98
  470.3 5.2 collective-permute-start
  476.5 409.3 %all-gather.17.cloned.1.call-start = ((), (), s32[]{:S(2)}) async-start(), calls=%async_computation.5 | async-start | bytes 2129920 | tf_op jit(solution)/shard_map/all_gather | solution.py:88
  889.4 24.6 %all-to-all-start.1 = ((bf16[64,2,128]{2,1,0:T(2,128)(2,1)}), bf16[64,2,128]{2,1,0:T(2,128)(2,1)S(1)}, u32[]{:S(2)}, u32[]{:S(2)}) async-start(bf16[64,2,128]{2,1,0:T(2,128)(2,1)} %bitcast.29), calls=%async_computation.1 | async-start | bytes 65536 | tf_op jit(solution)/shard_map/all_to_all | solution.py:99
Sparse Core Ops, SparseCore 0:
  11.6 144.2 all-gather.10
  159.3 136.7 all-gather.18
  305.0 136.9 all-gather.14
  460.0 140.6 all-gather.12
  604.0 136.7 all-gather.20
  748.8 136.9 all-gather.16
where the time goes:
time: 922 us
  waiting for transfers between devices  843 us (91%)
  starting transfers between devices  22.7 us (2%)
  matrix products  16.7 us (2%)
  local copies, waits for them, and re-layouts  14.9 us (2%)
  between operations  14.3 us (2%)
  other arithmetic  9.66 us (1%)
    all_gather x2, waiting for transfers between devices, advance(): queries = query_part(lax.all_gather(normed, 'mp', axis=0, tiled=True))  276 us
    all_gather x2, waiting for transfers between devices, branch(): projected = add_heads(lax.all_gather(attended, 'mp', axis=1, tiled=True))  274 us
    all_gather x2, waiting for transfers between devices, fetch(): return project(lax.all_gather(chosen(micro), 'mp', axis=1, tiled=True))  263 us
    all_to_all x2, waiting for transfers between devices, advance(): lax.all_to_all(branch(queries, key_values, slot_mask), 'mp', split_axis=0...  27.3 us
    all_to_all x2, starting transfers between devices, advance(): lax.all_to_all(branch(queries, key_values, slot_mask), 'mp', split_axis=0...  20.5 us
  transfers between devices with their start and end apart: 9, of which 9 were waited for; matrix products, arithmetic and copies ran while one was open for 1% of the time, Pallas kernels for 0%

commit v1 on v0

v1 whole, which is shorter than its diff:
```python
import functools

import jax
import jax.numpy as jnp
from jax import lax
from jax.experimental import pallas as pl
from jax.experimental.pallas import tpu as pltpu
from jax.sharding import PartitionSpec as P

MESH = pl.DeviceIdType.MESH

HD = 128
LAT = 64
IMG = 8
MB = 128
D = 8192
VD = 1280
NY = 4
NZ = 16
QUARTER = D // NY
HALF_VD = VD // 2

epsilon = 1e-05
negative_big = -1e30


def both_ways(edges):
    listed = []
    for reached, via in edges:
        listed.append((reached, via))
        if reached != NZ // 2:
            listed.append((-reached, -via))
    return listed


TREE = both_ways([(6, 0), (2, 0), (1, 0), (3, 2), (4, 2), (8, 6), (7, 6), (5, 6)])
STEPS = sorted({reached - via for reached, via in TREE})


def arrived(ref, sem):
    pltpu.make_async_copy(ref, ref, sem).wait()


class Gather:
    def __init__(self, place, block, send, recv):
        self.place, self.block, self.send, self.recv = place, block, send, recv
        self.copies, self.here = [], {0}

    def need(self, offset):
        if offset not in self.here:
            self.here.add(offset)
            z = self.place[2]
            arrived(self.block(lax.rem(z - offset + NZ, NZ)), self.recv(offset % NZ))

    def pass_on(self, edges):
        s, y, z = self.place
        for reached, via in edges:
            self.need(via)
            ref = self.block(lax.rem(z - via + NZ, NZ))
            copy = pltpu.make_async_remote_copy(
                src_ref=ref,
                dst_ref=ref,
                send_sem=self.send(reached % NZ),
                recv_sem=self.recv(reached % NZ),
                device_id=(s, y * NZ + lax.rem(z + reached - via + NZ, NZ)),
                device_id_type=MESH,
            )
            copy.start()
            self.copies.append(copy)

    def begin(self):
        self.pass_on([edge for edge in TREE if edge[1] == 0])

    def forward(self):
        self.pass_on([edge for edge in TREE if edge[1] != 0])

    def finish(self):
        for reached, _ in TREE:
            self.need(reached)

    def drain(self):
        for copy in self.copies:
            copy.wait_send()


def kernel(
    rows_ref, lat_ref, mask_ref, gain_ref, wq_ref, wkv_ref, wo_ref, alpha_ref,
    out_ref,
    wq_all, wo_all, wkv_all, entry, stripes, columns, first_blocks, blocks, lat_all,
    matrix, squares, partial, others, kv, relay_out, relay_in, out_cols, out_rows, out_pairs,
    local_sem, y_send, y_recv, w_send, w_recv, z_send, z_recv, l_send, l_recv, ly_send, ly_recv,
    c_send, c_recv, r_send, r_recv, n_send, n_recv, oz_send, oz_recv, oy_send, oy_recv,
):
    s = lax.axis_index("section")
    mp = lax.axis_index("mp")
    y, z = mp // NZ, lax.rem(mp, NZ)
    place = (s, y, z)

    def at_y(d):
        return (s, lax.rem(y + d, NY) * NZ + z)

    def at_z(d):
        return (s, y * NZ + lax.rem(z + d + NZ, NZ))

    following = (lax.rem(s + 1, 8), mp)
    previous = (lax.rem(s + 7, 8), mp)

    def send(src, dst, send_sem, recv_sem, device):
        copy = pltpu.make_async_remote_copy(
            src_ref=src, dst_ref=dst, send_sem=send_sem, recv_sem=recv_sem,
            device_id=device, device_id_type=MESH,
        )
        copy.start()
        return copy

    pending = []

    def quarter(ref, which):
        return ref.at[pl.ds(pl.multiple_of(which * QUARTER, QUARTER), QUARTER)]

    keeps = [
        pltpu.make_async_copy(quarter(wq_ref, y), wq_all.at[y], local_sem.at[0]),
        pltpu.make_async_copy(quarter(wo_ref, y), wo_all.at[y], local_sem.at[1]),
        pltpu.make_async_copy(wkv_ref.at[0], wkv_all.at[:, pl.ds(0, HD)], local_sem.at[2]),
        pltpu.make_async_copy(wkv_ref.at[1], wkv_all.at[:, pl.ds(HD, HD)], local_sem.at[3]),
    ]
    for copy in keeps:
        copy.start()

    barrier = pltpu.get_barrier_semaphore()
    greeted = [at_z(d) for d in STEPS] + [at_y(d) for d in (1, 2, 3)] + [following, previous]
    for device in greeted:
        pl.semaphore_signal(barrier, inc=1, device_id=device, device_id_type=MESH)
    pl.semaphore_wait(barrier, len(greeted))

    def entry_rows(which):
        return pl.ds(pl.multiple_of(which * 32, 32), 32)

    def swap_rows(k):
        for d in (2, 1, 3):
            pending.append(
                send(
                    rows_ref.at[k, lax.rem(y + d, NY)], entry.at[k, entry_rows(y)],
                    y_send.at[k, d], y_recv.at[k, d], at_y(d),
                )
            )

    def rows_here(k):
        entry[k, entry_rows(y)] = rows_ref[k, y]
        for d in (1, 2, 3):
            arrived(entry.at[k, entry_rows(lax.rem(y + NY - d, NY))], y_recv.at[k, d])
        for at in range(NZ):
            stripes[k, :, pl.ds(at * 128, 128)] = entry[k, pl.ds(at, 8, stride=NZ), :]

    def swap_weights(k, src, dst):
        for d in (2, 1, 3):
            pending.append(
                send(
                    quarter(src, lax.rem(y + d, NY)), dst.at[y],
                    w_send.at[k, d], w_recv.at[k, d], at_y(d),
                )
            )

    def weights_here(k, dst):
        keeps[k].wait()
        for d in (1, 2, 3):
            arrived(dst.at[lax.rem(y + NY - d, NY)], w_recv.at[k, d])

    swap_rows(0)
    lat_all[0, y, z] = lat_ref[0]
    lat_all[1, y, z] = lat_ref[1]
    lat_gathers = [
        Gather(
            place, lambda at, k=k: lat_all.at[k, y, at],
            lambda i, k=k: l_send.at[k, i], lambda i, k=k: l_recv.at[k, i],
        )
        for k in range(2)
    ]
    lat_gathers[0].begin()
    swap_weights(0, wq_ref, wq_all)

    def spread_lat(k):
        for d in (2, 1, 3):
            pending.append(
                send(
                    lat_all.at[k, y], lat_all.at[k, y],
                    ly_send.at[k, d], ly_recv.at[k, d], at_y(d),
                )
            )

    def lat_here(k):
        for d in (1, 2, 3):
            arrived(lat_all.at[k, lax.rem(y + NY - d, NY)], ly_recv.at[k, d])

    def make_kv(k):
        @pl.loop(0, 4)
        def _(part):
            held = lat_all[k, part].reshape(NZ * 16, HALF_VD)
            low = jnp.dot(held, wkv_all[:HALF_VD, :], preferred_element_type=jnp.float32)
            high = jnp.dot(held, wkv_all[HALF_VD:, :], preferred_element_type=jnp.float32)
            low = low.reshape(NZ, 16, 2 * HD)[:, :8]
            high = high.reshape(NZ, 16, 2 * HD)[:, 8:]
            made = (low + high).reshape(NZ * IMG, 2 * HD).astype(jnp.bfloat16)
            kv[pl.ds(pl.multiple_of(part * 128, 128), 128), :] = made

    gathers = [
        Gather(
            place,
            (lambda at: first_blocks.at[at]) if g == 0 else (lambda at, g=g: blocks.at[g - 1, at]),
            lambda i, g=g: z_send.at[g, i], lambda i, g=g: z_recv.at[g, i],
        )
        for g in range(4)
    ]

    rows_here(0)
    first_blocks[z] = jnp.concatenate(
        [stripes[0, :, pl.ds(0, 1024)], stripes[0, :, pl.ds(1024, 1024)]], axis=0
    ).astype(jnp.bfloat16)
    gathers[0].begin()
    lat_gathers[0].forward()
    swap_rows(1)
    gathers[0].forward()
    lat_gathers[0].finish()
    spread_lat(0)
    swap_weights(1, wo_ref, wo_all)
    gathers[0].finish()
    lat_gathers[1].begin()

    rows_here(1)

    def column_rows(which):
        return pl.ds(pl.multiple_of(which * 8, 8), 8)

    def lanes(which):
        return pl.ds(pl.multiple_of(which * 128, 128), 128)

    def start_columns(k):
        @pl.loop(1, NZ)
        def _(d):
            target = lax.rem(z + d, NZ)
            send(
                stripes.at[k, :, lanes(target)], columns.at[k, column_rows(z)],
                c_send.at[k, d], c_recv.at[k, d], at_z(d),
            )

        columns[k, column_rows(z), :] = stripes[k, :, lanes(z)]

    def columns_here(k):
        @pl.loop(1, NZ)
        def _(d):
            arrived(columns.at[k, column_rows(lax.rem(z + NZ - d, NZ))], c_recv.at[k, d])

    def columns_sent(k):
        @pl.loop(1, NZ)
        def _(d):
            ref = stripes.at[k, :, lanes(lax.rem(z + d, NZ))]
            pltpu.make_async_copy(ref, ref, c_send.at[k, d]).wait()

    gain_here = gain_ref[:, pl.ds(pl.multiple_of(y * QUARTER, QUARTER), QUARTER)]

    def matrix_of_rows():
        @pl.loop(0, NZ // 2)
        def _(pair):
            one = first_blocks[2 * pair].astype(jnp.float32)
            two = first_blocks[2 * pair + 1].astype(jnp.float32)
            total = jnp.zeros((16, 128), jnp.float32)
            where = pl.ds(pl.multiple_of(pair * 16, 16), 16)
            for half in range(2):
                part = jnp.concatenate([one[half * 8:half * 8 + 8], two[half * 8:half * 8 + 8]], axis=0)
                for lane in range(8):
                    cut = part[:, lane * 128:lane * 128 + 128]
                    total = total + cut * cut
                gain_part = gain_here[:, half * 1024:half * 1024 + 1024]
                matrix[where, pl.ds(half * 1024, 1024)] = (part * gain_part).astype(jnp.bfloat16)
            squares[where, :] = total

    def matrix_of_blocks(g):
        squares[...] = jnp.zeros_like(squares)
        for at in range(NZ):
            block = blocks[g - 1, at].astype(jnp.float32)
            squares[...] += block * block
            matrix[:, pl.ds(at * 128, 128)] = (
                block * gain_here[:, at * 128:at * 128 + 128]
            ).astype(jnp.bfloat16)

    def matrix_plain(g):
        for at in range(NZ):
            matrix[:, pl.ds(at * 128, 128)] = blocks[g - 1, at]

    def start_sums(g, weights, with_squares):
        rows = MB + 8 if with_squares else MB
        if with_squares:
            row = jnp.sum(squares[...].T, axis=0, keepdims=True)
            row = jnp.broadcast_to(row, (8, 128))
        for d in (2, 1, 3, 0):
            target = lax.rem(y + d, NY)
            partial[g, target, pl.ds(0, MB), :] = jnp.dot(
                matrix[...], weights[target], preferred_element_type=jnp.float32
            )
            if with_squares:
                partial[g, target, pl.ds(MB, 8), :] = row
            if d:
                pending.append(
                    send(
                        partial.at[g, target, pl.ds(0, rows)], others.at[g, y, pl.ds(0, rows)],
                        r_send.at[g, d], r_recv.at[g, d], at_y(d),
                    )
                )

    def sums(g, with_squares):
        rows = MB + 8 if with_squares else MB
        for d in (1, 2, 3):
            arrived(others.at[g, lax.rem(y + NY - d, NY), pl.ds(0, rows)], r_recv.at[g, d])
        total = partial[g, y, pl.ds(0, rows), :]
        for d in (1, 2, 3):
            total = total + others[g, lax.rem(y + NY - d, NY), pl.ds(0, rows), :]
        return total

    def attend(k, total):
        row = jnp.broadcast_to(total[MB:MB + 1, :], (128, 128))
        scale = lax.rsqrt(row.T * (1.0 / D) + epsilon)
        queries = (total[:MB] * scale).astype(jnp.bfloat16)
        scores = lax.dot_general(
            queries, kv[:, :HD], (((1,), (1,)), ((), ())), preferred_element_type=jnp.float32
        ) * HD ** (-0.5)
        seen = mask_ref[k]
        visible = jnp.concatenate([seen] * 4, axis=1) > 0
        seen_any = jnp.max(seen, axis=1, keepdims=True) > 0
        largest = jnp.max(jnp.where(visible, scores, negative_big), axis=1, keepdims=True)
        largest = jnp.where(seen_any, largest, 0.0)
        expanded = jnp.where(visible, jnp.exp(jnp.where(visible, scores - largest, 0.0)), 0.0)
        totals = jnp.sum(expanded, axis=1, keepdims=True)
        totals = jnp.where(seen_any, totals, 1.0)
        probs = (expanded / totals).astype(jnp.bfloat16)
        return jnp.dot(probs, kv[:, HD:], preferred_element_type=jnp.float32).astype(jnp.bfloat16)

    gate = jnp.tanh(alpha_ref[...])

    def block_out(total, hidden):
        branch = (total * gate).astype(jnp.bfloat16).astype(jnp.float32)
        return (hidden + branch).astype(jnp.bfloat16)

    def start_out(k, made):
        out_cols[k] = made.astype(jnp.float32)

        @pl.loop(1, NZ)
        def _(d):
            send(
                out_cols.at[k, column_rows(lax.rem(z + d, NZ))], out_rows.at[k, column_rows(z)],
                oz_send.at[k, d], oz_recv.at[k, d], at_z(d),
            )

        out_rows[k, column_rows(z), :] = out_cols[k, column_rows(z), :]

    def turn_out(k):
        @pl.loop(1, NZ)
        def _(d):
            arrived(out_rows.at[k, column_rows(lax.rem(z + NZ - d, NZ))], oz_recv.at[k, d])

        for target in range(NY):
            for token in range(2):
                out_pairs[k, target, token] = out_rows[k, pl.ds(2 * target + token, NZ, stride=8), :]
        for d in (2, 1, 3):
            pending.append(
                send(
                    out_pairs.at[k, lax.rem(y + d, NY)], out_ref.at[k, y],
                    oy_send.at[k, d], oy_recv.at[k, d], at_y(d),
                )
            )
        out_ref[k, y] = out_pairs[k, y]

    def out_here(k):
        for d in (1, 2, 3):
            arrived(out_ref.at[k, lax.rem(y + NY - d, NY)], oy_recv.at[k, d])

    def out_sent(k):
        @pl.loop(1, NZ)
        def _(d):
            ref = out_cols.at[k, column_rows(lax.rem(z + d, NZ))]
            pltpu.make_async_copy(ref, ref, oz_send.at[k, d]).wait()

    matrix_of_rows()
    weights_here(0, wq_all)
    start_sums(0, wq_all, True)
    keeps[2].wait()
    keeps[3].wait()
    lat_here(0)
    make_kv(0)
    blocks[0, z] = attend(0, sums(0, True))
    gathers[1].begin()
    lat_gathers[1].forward()
    start_columns(0)
    start_columns(1)
    gathers[1].forward()
    lat_gathers[1].finish()
    spread_lat(1)
    columns_here(0)
    columns_here(1)
    gathers[1].finish()
    matrix_plain(1)
    weights_here(1, wo_all)
    start_sums(1, wo_all, False)
    lat_here(1)
    make_kv(1)
    made = block_out(sums(1, False), columns[0])
    relay_out[...] = made
    pending.append(send(relay_out, relay_in, n_send.at[0], n_recv.at[0], following))
    arrived(relay_in, n_recv.at[0])

    entering = jnp.where(s == 0, columns[1], relay_in[...].astype(jnp.float32))
    blocks[1, z] = entering.astype(jnp.bfloat16)
    gathers[2].begin()
    start_out(0, made)
    gathers[2].forward()
    gathers[2].finish()
    matrix_of_blocks(2)
    start_sums(2, wq_all, True)
    turn_out(0)
    blocks[2, z] = attend(1, sums(2, True))
    gathers[3].begin()
    gathers[3].forward()
    gathers[3].finish()
    matrix_plain(3)
    start_sums(3, wo_all, False)
    start_out(1, block_out(sums(3, False), blocks[1, z].astype(jnp.float32)))
    turn_out(1)
    out_here(0)
    out_here(1)

    for gather in gathers + lat_gathers:
        gather.drain()
    for copy in pending:
        copy.wait_send()
    for k in range(2):
        columns_sent(k)
        out_sent(k)


def local(section_in, fresh, latents, image_order, token_mask, norm_gain, wq, wkv, wo, alpha):
    section = lax.axis_index("section")
    first_micro = 7 - section

    rows = jnp.stack([section_in[0], fresh]).reshape(2, 2, NY, NZ, 128)
    rows = rows.transpose(0, 2, 1, 3, 4).reshape(2, NY, 32, 128).astype(jnp.float32)

    image_ids = lax.dynamic_slice_in_dim(image_order, first_micro * IMG, 2 * IMG)
    picked = jnp.take(latents[:, 0], image_ids, axis=0).reshape(2, IMG, 2, HALF_VD)
    picked = picked.transpose(0, 2, 1, 3).reshape(2, 16, HALF_VD)

    seen = lax.dynamic_slice_in_dim(token_mask, first_micro, 2).reshape(2, NY, NZ, 2, IMG)
    seen = seen.transpose(0, 2, 1, 3, 4).reshape(2, MB, IMG).astype(jnp.float32)
    seen = jnp.tile(seen, (1, 1, 128 // IMG))

    vmem = pl.BlockSpec(memory_space=pltpu.VMEM)
    hbm = pl.BlockSpec(memory_space=pl.ANY)
    bf16, f32 = jnp.bfloat16, jnp.float32
    dma = pltpu.SemaphoreType.DMA
    out = pl.pallas_call(
        kernel,
        out_shape=jax.ShapeDtypeStruct((2, NY, 2, NZ, 128), f32),
        in_specs=[vmem, vmem, vmem, vmem, hbm, hbm, hbm, vmem],
        out_specs=vmem,
        scratch_shapes=[
            pltpu.VMEM((NY, QUARTER, HD), bf16),
            pltpu.VMEM((NY, QUARTER, HD), bf16),
            pltpu.VMEM((VD, 2 * HD), bf16),
            pltpu.VMEM((2, MB, 128), f32),
            pltpu.VMEM((2, 8, QUARTER), f32),
            pltpu.VMEM((2, MB, 128), f32),
            pltpu.VMEM((NZ, 16, 1024), bf16),
            pltpu.VMEM((3, NZ, MB, 128), bf16),
            pltpu.VMEM((2, NY, NZ, 16, HALF_VD), bf16),
            pltpu.VMEM((MB, QUARTER), bf16),
            pltpu.VMEM((MB, 128), f32),
            pltpu.VMEM((4, NY, MB + 8, 128), f32),
            pltpu.VMEM((4, NY, MB + 8, 128), f32),
            pltpu.VMEM((LAT * IMG, 2 * HD), bf16),
            pltpu.VMEM((MB, 128), bf16),
            pltpu.VMEM((MB, 128), bf16),
            pltpu.VMEM((2, MB, 128), f32),
            pltpu.VMEM((2, MB, 128), f32),
            pltpu.VMEM((2, NY, 2, NZ, 128), f32),
            dma((4,)),
            dma((2, 4)), dma((2, 4)),
            dma((2, 4)), dma((2, 4)),
            dma((4, NZ)), dma((4, NZ)),
            dma((2, NZ)), dma((2, NZ)),
            dma((2, 4)), dma((2, 4)),
            dma((2, NZ)), dma((2, NZ)),
            dma((4, 4)), dma((4, 4)),
            dma((1,)), dma((1,)),
            dma((2, NZ)), dma((2, NZ)),
            dma((2, 4)), dma((2, 4)),
        ],
        compiler_params=pltpu.CompilerParams(
            collective_id=0, has_side_effects=True, vmem_limit_bytes=48 * 2**20
        ),
    )(
        rows, picked, seen, norm_gain.astype(f32), wq[0], wkv[0], wo[0], alpha,
    )
    out = out.transpose(0, 2, 1, 3, 4).reshape(2, 1, 2, D).astype(bf16)
    return out[0], out[1]


def solution(mesh):
    in_specs = (
        P("section", "mp", None),
        P("mp", None),
        P(None, "mp", None),
        P(),
        P(),
        P("section", None),
        P("section", None, "mp"),
        P("section", None, None, "mp"),
        P("section", None, "mp"),
        P("section", "mp"),
    )
    out_specs = (P("section", "mp", None), P("section", "mp", None))
    return jax.shard_map(local, mesh=mesh, in_specs=in_specs, out_specs=out_specs, check_vma=False)
```

time: 922 us -> 179 us (0.19)
  waiting for transfers between devices: 843 us -> 0 us
  Pallas kernels: 0 us -> 167 us
  starting transfers between devices: 22.7 us -> 0 us
  matrix products: 16.7 us -> 0 us
  between operations: 14.3 us -> 0.75 us
    all_gather x6 -> x0, waiting for transfers between devices: 813 us -> none  [the longest x2 276 us: advance(): queries = query_part(lax.all_gather(normed, 'mp', axis=0, tiled=True))]
    pallas_call x0 -> x1, Pallas kernels: none -> 167 us  [local(): pl.pallas_call(kernel, out_shape=jax.ShapeDtypeStruct((2, NY, 2, NZ, 128)...]
    all_to_all x2 -> x0, waiting for transfers between devices: 27.3 us -> none  [advance(): lax.all_to_all(branch(queries, key_values, slot_mask), 'mp', split_axis=0...]
    all_to_all x2 -> x0, starting transfers between devices: 20.5 us -> none  [advance(): lax.all_to_all(branch(queries, key_values, slot_mask), 'mp', split_axis=0...]
    dot_general x8 -> x0, matrix products: 16.7 us -> none  [the longest x2 7.18 us: add_heads(): return jnp.dot(piece, proj_out, preferred_element_type=jnp.float32)]
  transfers between devices with their start and end apart: 9 -> 0, of which waited for: 9 -> 0; matrix products, arithmetic and copies ran while one was open for 1% -> 0% of each run, Pallas kernels for 0% -> 0%
where the time goes in v1:
time: 179 us
  Pallas kernels  167 us (93%)
  local copies, waits for them, and re-layouts  8.56 us (5%)
  other arithmetic  2.33 us (1%)
    pallas_call x1, Pallas kernels, local(): pl.pallas_call(kernel, out_shape=jax.ShapeDtypeStruct((2, NY, 2, NZ, 128)...  167 us
    unnamed x12, local copies, waits for them, and re-layouts  6.27 us

profile of v1, /device:TPU:6, one launch (start us, length us, event | category | flops | bytes accessed | tf_op | source)
XLA Modules:
  0.0 178.9 jit_solution(580873265922513789)
XLA Ops:
  0.6 0.0 copy-start
  0.6 0.0 copy-start.3
  0.7 0.9 copy-done
  1.6 0.7 compare_and_fusion
  2.3 0.1 broadcast_in_dim.14
  2.4 0.7 dynamic-slice_convert_fusion
  3.1 0.8 copy.23
  3.8 0.8 copy.24
  4.6 0.8 convert_element_type.48.gain_ref
  5.4 0.6 gather_fusion
  6.0 0.1 select_bitcast_fusion.lat_ref
  6.1 0.1 copy.16
  6.3 0.1 copy.18
  6.4 0.1 copy.19.mask_ref
  6.5 0.0 copy-done.3
  6.5 0.0 copy-start.1
  6.5 1.6 copy-done.1
  8.1 0.0 copy-start.2
  8.1 1.6 copy-done.2
  9.7 0.0 copy-start.4
  9.7 0.7 copy-done.4
  10.3 167.3 %shard_map.113 = f32[2,4,2,16,128]{4,3,2,1,0:T(8,128)S(1)} custom-call(f32[2,4,32,128]{3,2,1,0:T(8,128)S(1)} %bitcast.35, bf16[2,16,640]{2,1,0:T(8,128)(2,1)S(1)} %select_bitcast_fusion.lat_ref, f32[2,128,128]{2,1,0:T(8,128)S(1)} %copy.19.mask_ref, f32[1,8192]{1,0:T(1,128)S(1)} %convert_element_type.48.gain_ref, bf16[8192,128]{1,0:T(8,128)(2,1)S(1)} %bitcast.32, ...), custom_call_target="tpu_custom_call" | custom-call | tf_op jit(solution)/shard_map/pallas_call | solution.py:458
  177.6 0.6 squeeze.23
  178.3 0.6 squeeze.22
  (8 shorter events, 0.1 us)
Async XLA Ops:
  0.6 0.9 copy-start
  0.6 5.8 %copy-start.3 = (bf16[1,2,1280,128]{3,2,1,0:T(8,128)(2,1)S(1)}, bf16[1,2,1280,128]{3,2,1,0:T(8,128)(2,1)}, u32[]{:S(2)}) copy-start(bf16[1,2,1280,128]{3,2,1,0:T(8,128)(2,1)} %param.17) | copy-start | bytes 1966084
  6.5 1.6 copy-start.1
  8.1 1.6 copy-start.2
  9.7 0.7 copy-start.4

commit v2 on v1

--- a/solution.py
+++ b/solution.py
@@ -34,7 +34,8 @@
 
 
 TREE = both_ways([(6, 0), (2, 0), (1, 0), (3, 2), (4, 2), (8, 6), (7, 6), (5, 6)])
-STEPS = sorted({reached - via for reached, via in TREE})
+LEAN = both_ways([(4, 0), (1, 0), (2, 1), (3, 4), (5, 4), (6, 5), (7, 6), (8, 7)])
+STEPS = sorted({reached - via for tree in (TREE, LEAN) for reached, via in tree})
 
 
 def arrived(ref, sem):
@@ -42,54 +43,49 @@
 
 
 class Gather:
-    def __init__(self, place, block, send, recv):
-        self.place, self.block, self.send, self.recv = place, block, send, recv
-        self.copies, self.here = [], {0}
+    def __init__(self, place, block, send, recv, tree):
+        self.place, self.block, self.send, self.recv, self.tree = place, block, send, recv, tree
+        self.here = {0}
+
+    def origin(self, offset):
+        return self.block(lax.rem(self.place[2] - offset + NZ, NZ))
 
     def need(self, offset):
         if offset not in self.here:
             self.here.add(offset)
-            z = self.place[2]
-            arrived(self.block(lax.rem(z - offset + NZ, NZ)), self.recv(offset % NZ))
-
-    def pass_on(self, edges):
+            arrived(self.origin(offset), self.recv(offset % NZ))
+
+    def pass_on(self, *vias):
         s, y, z = self.place
-        for reached, via in edges:
-            self.need(via)
-            ref = self.block(lax.rem(z - via + NZ, NZ))
-            copy = pltpu.make_async_remote_copy(
-                src_ref=ref,
-                dst_ref=ref,
-                send_sem=self.send(reached % NZ),
-                recv_sem=self.recv(reached % NZ),
-                device_id=(s, y * NZ + lax.rem(z + reached - via + NZ, NZ)),
-                device_id_type=MESH,
-            )
-            copy.start()
-            self.copies.append(copy)
-
-    def begin(self):
-        self.pass_on([edge for edge in TREE if edge[1] == 0])
-
-    def forward(self):
-        self.pass_on([edge for edge in TREE if edge[1] != 0])
+        for reached, via in self.tree:
+            if abs(via) in vias:
+                self.need(via)
+                pltpu.make_async_remote_copy(
+                    src_ref=self.origin(via),
+                    dst_ref=self.origin(via),
+                    send_sem=self.send(reached % NZ),
+                    recv_sem=self.recv(reached % NZ),
+                    device_id=(s, y * NZ + lax.rem(z + reached - via + NZ, NZ)),
+                    device_id_type=MESH,
+                ).start()
 
     def finish(self):
-        for reached, _ in TREE:
+        for reached, _ in self.tree:
             self.need(reached)
 
-    def drain(self):
-        for copy in self.copies:
-            copy.wait_send()
+    def drain(self, first=True):
+        for reached, via in self.tree:
+            if via or first:
+                arrived(self.origin(via), self.send(reached % NZ))
 
 
 def kernel(
-    rows_ref, lat_ref, mask_ref, gain_ref, wq_ref, wkv_ref, wo_ref, alpha_ref,
+    section_ref, fresh_ref, latents_ref, order_ref, mask_ref, gain_ref, wq_ref, wkv_ref, wo_ref, alpha_ref,
     out_ref,
-    wq_all, wo_all, wkv_all, entry, stripes, columns, first_blocks, blocks, lat_all,
-    matrix, squares, partial, others, kv, relay_out, relay_in, out_cols, out_rows, out_pairs,
-    local_sem, y_send, y_recv, w_send, w_recv, z_send, z_recv, l_send, l_recv, ly_send, ly_recv,
-    c_send, c_recv, r_send, r_recv, n_send, n_recv, oz_send, oz_recv, oy_send, oy_recv,
+    wq_all, wo_all, wkv_all, rows32, entry, stripes, columns, first_blocks, blocks, lat_all, seen_all, gain32,
+    matrix, squares, partial, others, kv, relay_out, out_cols, out_rows, out_pairs,
+    local_sem, y_send, y_recv, w_send, w_recv, z_send, z_recv, l_send, l_recv, ly_send, ly_recv, lr_send, lr_recv,
+    c_send, c_recv, r_send, r_recv, n_send, n_recv, k_sem, oz_send, oz_recv, oy_send, oy_recv,
 ):
     s = lax.axis_index("section")
     mp = lax.axis_index("mp")
@@ -114,6 +110,9 @@
         return copy
 
     pending = []
+
+    def signal(sem, device):
+        pl.semaphore_signal(sem, inc=1, device_id=device, device_id_type=MESH)
 
     def quarter(ref, which):
         return ref.at[pl.ds(pl.multiple_of(which * QUARTER, QUARTER), QUARTER)]
@@ -130,27 +129,48 @@
     barrier = pltpu.get_barrier_semaphore()
     greeted = [at_z(d) for d in STEPS] + [at_y(d) for d in (1, 2, 3)] + [following, previous]
     for device in greeted:
-        pl.semaphore_signal(barrier, inc=1, device_id=device, device_id_type=MESH)
+        signal(barrier, device)
+
+    rows32[0] = section_ref[...].astype(jnp.float32)
+    rows32[1] = fresh_ref[...].astype(jnp.float32)
+    image_row = lax.broadcasted_iota(jnp.int32, (2 * IMG, 72), 0)
+    image_lane = lax.broadcasted_iota(jnp.int32, (2 * IMG, 72), 1)
+    chosen = jnp.zeros((2 * IMG, 72), jnp.float32)
+    for i in range(2 * IMG):
+        image = order_ref[(7 - s) * IMG + i]
+        chosen = jnp.where((image_row == i) & (image_lane == image), 1.0, chosen)
+    picked = jnp.dot(
+        chosen.astype(jnp.bfloat16), latents_ref[...], preferred_element_type=jnp.float32
+    )
+
+    def keep_lat(k):
+        rows = picked[k * IMG:k * IMG + IMG]
+        lat_all[k, z, y] = jnp.concatenate([rows[:, :HALF_VD], rows[:, HALF_VD:]], axis=0).astype(jnp.bfloat16)
+
+    keep_lat(0)
+
+    @pl.when(s == 0)
+    def _():
+        keep_lat(1)
+
     pl.semaphore_wait(barrier, len(greeted))
-
-    def entry_rows(which):
-        return pl.ds(pl.multiple_of(which * 32, 32), 32)
 
     def swap_rows(k):
         for d in (2, 1, 3):
+            target = lax.rem(y + d, NY)
             pending.append(
                 send(
-                    rows_ref.at[k, lax.rem(y + d, NY)], entry.at[k, entry_rows(y)],
+                    rows32.at[k, :, pl.ds(pl.multiple_of(target * QUARTER, QUARTER), QUARTER)], entry.at[k, y],
                     y_send.at[k, d], y_recv.at[k, d], at_y(d),
                 )
             )
 
     def rows_here(k):
-        entry[k, entry_rows(y)] = rows_ref[k, y]
+        entry[k, y] = rows32[k, :, pl.ds(pl.multiple_of(y * QUARTER, QUARTER), QUARTER)]
         for d in (1, 2, 3):
-            arrived(entry.at[k, entry_rows(lax.rem(y + NY - d, NY))], y_recv.at[k, d])
-        for at in range(NZ):
-            stripes[k, :, pl.ds(at * 128, 128)] = entry[k, pl.ds(at, 8, stride=NZ), :]
+            arrived(entry.at[k, lax.rem(y + NY - d, NY)], y_recv.at[k, d])
+        for at in range(NY):
+            stripes[k, pl.ds(2 * at, 2), :] = entry[k, at]
 
     def swap_weights(k, src, dst):
         for d in (2, 1, 3):
@@ -166,36 +186,52 @@
         for d in (1, 2, 3):
             arrived(dst.at[lax.rem(y + NY - d, NY)], w_recv.at[k, d])
 
-    swap_rows(0)
-    lat_all[0, y, z] = lat_ref[0]
-    lat_all[1, y, z] = lat_ref[1]
     lat_gathers = [
         Gather(
-            place, lambda at, k=k: lat_all.at[k, y, at],
-            lambda i, k=k: l_send.at[k, i], lambda i, k=k: l_recv.at[k, i],
+            place, (lambda at: lat_all.at[1, at, y]) if k else (lambda at: lat_all.at[0, at]),
+            lambda i, k=k: l_send.at[k, i], lambda i, k=k: l_recv.at[k, i], TREE if k else LEAN,
         )
         for k in range(2)
     ]
-    lat_gathers[0].begin()
+
+    def lat_part(k, which):
+        return lat_all.at[k, :, which] if k else lat_all.at[k, z, which]
+
+    def swap_lat(k):
+        for d in (2, 1, 3):
+            send(lat_part(k, y), lat_part(k, y), ly_send.at[k, d], ly_recv.at[k, d], at_y(d))
+
+    def lat_swapped(k):
+        for d in (1, 2, 3):
+            arrived(lat_part(k, lax.rem(y + NY - d, NY)), ly_recv.at[k, d])
+
+    def lat_swap_sent(k):
+        for d in (1, 2, 3):
+            arrived(lat_part(k, y), ly_send.at[k, d])
+
+    swap_rows(0)
+    swap_lat(0)
     swap_weights(0, wq_ref, wq_all)
-
-    def spread_lat(k):
-        for d in (2, 1, 3):
-            pending.append(
-                send(
-                    lat_all.at[k, y], lat_all.at[k, y],
-                    ly_send.at[k, d], ly_recv.at[k, d], at_y(d),
-                )
-            )
-
-    def lat_here(k):
-        for d in (1, 2, 3):
-            arrived(lat_all.at[k, lax.rem(y + NY - d, NY)], ly_recv.at[k, d])
+    gain32[...] = gain_ref[...].astype(jnp.float32)
+
+    row_at = lax.broadcasted_iota(jnp.int32, (MB, MB), 0)
+    lane_at = lax.broadcasted_iota(jnp.int32, (MB, MB), 1)
+    token = ((row_at >> 1) & 3) * 32 + (row_at >> 3) * 2 + (row_at & 1)
+    reorder = jnp.where(lane_at == token, 1.0, 0.0).astype(jnp.bfloat16)
+    slot_at = lax.broadcasted_iota(jnp.int32, (IMG, MB), 0)
+    slot_lane = lax.broadcasted_iota(jnp.int32, (IMG, MB), 1)
+    repeat = jnp.where((slot_lane & 7) == slot_at, 1.0, 0.0).astype(jnp.bfloat16)
+    for k in range(2):
+        slots = mask_ref[7 - s + k].astype(jnp.float32).astype(jnp.bfloat16)
+        slots = lax.dot_general(
+            reorder, slots, (((1,), (1,)), ((), ())), preferred_element_type=jnp.float32
+        )
+        seen_all[k] = jnp.dot(slots.astype(jnp.bfloat16), repeat, preferred_element_type=jnp.float32)
 
     def make_kv(k):
         @pl.loop(0, 4)
         def _(part):
-            held = lat_all[k, part].reshape(NZ * 16, HALF_VD)
+            held = lat_all[k, pl.ds(part * 4, 4)].reshape(NZ * 16, HALF_VD)
             low = jnp.dot(held, wkv_all[:HALF_VD, :], preferred_element_type=jnp.float32)
             high = jnp.dot(held, wkv_all[HALF_VD:, :], preferred_element_type=jnp.float32)
             low = low.reshape(NZ, 16, 2 * HD)[:, :8]
@@ -207,7 +243,7 @@
         Gather(
             place,
             (lambda at: first_blocks.at[at]) if g == 0 else (lambda at, g=g: blocks.at[g - 1, at]),
-            lambda i, g=g: z_send.at[g, i], lambda i, g=g: z_recv.at[g, i],
+            lambda i, g=g: z_send.at[g, i], lambda i, g=g: z_recv.at[g, i], TREE,
         )
         for g in range(4)
     ]
@@ -216,17 +252,16 @@
     first_blocks[z] = jnp.concatenate(
         [stripes[0, :, pl.ds(0, 1024)], stripes[0, :, pl.ds(1024, 1024)]], axis=0
     ).astype(jnp.bfloat16)
-    gathers[0].begin()
-    lat_gathers[0].forward()
+    gathers[0].pass_on(0)
+    lat_swapped(0)
+    lat_gathers[0].pass_on(0)
     swap_rows(1)
-    gathers[0].forward()
-    lat_gathers[0].finish()
-    spread_lat(0)
-    swap_weights(1, wo_ref, wo_all)
+    gathers[0].pass_on(2, 6)
+    lat_gathers[0].pass_on(1, 4)
+    rows_here(1)
     gathers[0].finish()
-    lat_gathers[1].begin()
-
-    rows_here(1)
+    signal(k_sem, previous)
+    lat_gathers[0].pass_on(5)
 
     def column_rows(which):
         return pl.ds(pl.multiple_of(which * 8, 8), 8)
@@ -256,7 +291,7 @@
             ref = stripes.at[k, :, lanes(lax.rem(z + d, NZ))]
             pltpu.make_async_copy(ref, ref, c_send.at[k, d]).wait()
 
-    gain_here = gain_ref[:, pl.ds(pl.multiple_of(y * QUARTER, QUARTER), QUARTER)]
+    gain_here = gain32[:, pl.ds(pl.multiple_of(y * QUARTER, QUARTER), QUARTER)]
 
     def matrix_of_rows():
         @pl.loop(0, NZ // 2)
@@ -323,7 +358,7 @@
         scores = lax.dot_general(
             queries, kv[:, :HD], (((1,), (1,)), ((), ())), preferred_element_type=jnp.float32
         ) * HD ** (-0.5)
-        seen = mask_ref[k]
+        seen = seen_all[k]
         visible = jnp.concatenate([seen] * 4, axis=1) > 0
         seen_any = jnp.max(seen, axis=1, keepdims=True) > 0
         largest = jnp.max(jnp.where(visible, scores, negative_big), axis=1, keepdims=True)
@@ -382,43 +417,103 @@
     matrix_of_rows()
     weights_here(0, wq_all)
     start_sums(0, wq_all, True)
+    swap_weights(1, wo_ref, wo_all)
+    lat_gathers[0].pass_on(6, 7)
     keeps[2].wait()
     keeps[3].wait()
-    lat_here(0)
+    lat_gathers[0].finish()
     make_kv(0)
     blocks[0, z] = attend(0, sums(0, True))
-    gathers[1].begin()
-    lat_gathers[1].forward()
+    gathers[1].pass_on(0)
+
+    @pl.when(s < 7)
+    def _():
+        send(lat_all.at[0], lat_all.at[1], lr_send.at[0], lr_recv.at[0], following)
+
     start_columns(0)
     start_columns(1)
-    gathers[1].forward()
-    lat_gathers[1].finish()
-    spread_lat(1)
+
+    @pl.when(s == 0)
+    def _():
+        lat_gathers[1].pass_on(0)
+
+    gathers[1].pass_on(2, 6)
     columns_here(0)
     columns_here(1)
     gathers[1].finish()
+
+    @pl.when(s == 0)
+    def _():
+        lat_gathers[1].pass_on(2, 6)
+
     matrix_plain(1)
     weights_here(1, wo_all)
     start_sums(1, wo_all, False)
-    lat_here(1)
-    make_kv(1)
+    pl.semaphore_wait(k_sem, 1)
+
+    @pl.when(s == 0)
+    def _():
+        lat_gathers[1].finish()
+
     made = block_out(sums(1, False), columns[0])
     relay_out[...] = made
-    pending.append(send(relay_out, relay_in, n_send.at[0], n_recv.at[0], following))
-    arrived(relay_in, n_recv.at[0])
-
-    entering = jnp.where(s == 0, columns[1], relay_in[...].astype(jnp.float32))
-    blocks[1, z] = entering.astype(jnp.bfloat16)
-    gathers[2].begin()
+
+    hops = [reached for reached, via in TREE if via == 0]
+
+    @pl.when(s < 7)
+    def _():
+        for hop in hops:
+            send(
+                relay_out, blocks.at[1, z], z_send.at[2, hop % NZ], z_recv.at[2, hop % NZ],
+                (s + 1, y * NZ + lax.rem(z + hop + NZ, NZ)),
+            )
+        send(relay_out, blocks.at[1, z], n_send.at[0], n_recv.at[0], following)
+
+    @pl.when(s == 0)
+    def _():
+        blocks[1, z] = columns[1].astype(jnp.bfloat16)
+        for hop in hops:
+            send(
+                blocks.at[1, z], blocks.at[1, z], z_send.at[3, hop % NZ], z_recv.at[2, hop % NZ],
+                at_z(hop),
+            )
+
     start_out(0, made)
-    gathers[2].forward()
+
+    @pl.when(s == 0)
+    def _():
+        swap_lat(1)
+
+    gathers[2].pass_on(2, 6)
+
+    @pl.when(s > 0)
+    def _():
+        arrived(blocks.at[1, z], n_recv.at[0])
+
     gathers[2].finish()
     matrix_of_blocks(2)
     start_sums(2, wq_all, True)
+
     turn_out(0)
+
+    @pl.when(s == 0)
+    def _():
+        lat_swapped(1)
+
+    @pl.when(s > 0)
+    def _():
+        arrived(lat_all.at[1], lr_recv.at[0])
+
+    make_kv(1)
     blocks[2, z] = attend(1, sums(2, True))
-    gathers[3].begin()
-    gathers[3].forward()
+
+    @pl.when(s == 0)
+    def _():
+        for hop in hops:
+            arrived(blocks.at[1, z], z_send.at[3, hop % NZ])
+
+    gathers[3].pass_on(0)
+    gathers[3].pass_on(2, 6)
     gathers[3].finish()
     matrix_plain(3)
     start_sums(3, wo_all, False)
@@ -427,8 +522,25 @@
     out_here(0)
     out_here(1)
 
-    for gather in gathers + lat_gathers:
-        gather.drain()
+    gathers[0].drain()
+    gathers[1].drain()
+    gathers[2].drain(False)
+    gathers[3].drain()
+    lat_gathers[0].drain()
+    lat_swap_sent(0)
+
+    @pl.when(s == 0)
+    def _():
+        lat_swap_sent(1)
+        lat_gathers[1].drain()
+
+    @pl.when(s < 7)
+    def _():
+        for hop in hops:
+            arrived(relay_out, z_send.at[2, hop % NZ])
+        arrived(relay_out, n_send.at[0])
+        arrived(lat_all.at[0], lr_send.at[0])
+
     for copy in pending:
         copy.wait_send()
     for k in range(2):
@@ -437,45 +549,34 @@
 
 
 def local(section_in, fresh, latents, image_order, token_mask, norm_gain, wq, wkv, wo, alpha):
-    section = lax.axis_index("section")
-    first_micro = 7 - section
-
-    rows = jnp.stack([section_in[0], fresh]).reshape(2, 2, NY, NZ, 128)
-    rows = rows.transpose(0, 2, 1, 3, 4).reshape(2, NY, 32, 128).astype(jnp.float32)
-
-    image_ids = lax.dynamic_slice_in_dim(image_order, first_micro * IMG, 2 * IMG)
-    picked = jnp.take(latents[:, 0], image_ids, axis=0).reshape(2, IMG, 2, HALF_VD)
-    picked = picked.transpose(0, 2, 1, 3).reshape(2, 16, HALF_VD)
-
-    seen = lax.dynamic_slice_in_dim(token_mask, first_micro, 2).reshape(2, NY, NZ, 2, IMG)
-    seen = seen.transpose(0, 2, 1, 3, 4).reshape(2, MB, IMG).astype(jnp.float32)
-    seen = jnp.tile(seen, (1, 1, 128 // IMG))
-
     vmem = pl.BlockSpec(memory_space=pltpu.VMEM)
+    smem = pl.BlockSpec(memory_space=pltpu.SMEM)
     hbm = pl.BlockSpec(memory_space=pl.ANY)
     bf16, f32 = jnp.bfloat16, jnp.float32
     dma = pltpu.SemaphoreType.DMA
     out = pl.pallas_call(
         kernel,
         out_shape=jax.ShapeDtypeStruct((2, NY, 2, NZ, 128), f32),
-        in_specs=[vmem, vmem, vmem, vmem, hbm, hbm, hbm, vmem],
+        in_specs=[vmem, vmem, vmem, smem, vmem, vmem, hbm, hbm, hbm, vmem],
         out_specs=vmem,
         scratch_shapes=[
             pltpu.VMEM((NY, QUARTER, HD), bf16),
             pltpu.VMEM((NY, QUARTER, HD), bf16),
             pltpu.VMEM((VD, 2 * HD), bf16),
-            pltpu.VMEM((2, MB, 128), f32),
+            pltpu.VMEM((2, 2, D), f32),
+            pltpu.VMEM((2, NY, 2, QUARTER), f32),
             pltpu.VMEM((2, 8, QUARTER), f32),
             pltpu.VMEM((2, MB, 128), f32),
             pltpu.VMEM((NZ, 16, 1024), bf16),
             pltpu.VMEM((3, NZ, MB, 128), bf16),
-            pltpu.VMEM((2, NY, NZ, 16, HALF_VD), bf16),
+            pltpu.VMEM((2, NZ, NY, 16, HALF_VD), bf16),
+            pltpu.VMEM((2, MB, 128), f32),
+            pltpu.VMEM((1, D), f32),
             pltpu.VMEM((MB, QUARTER), bf16),
             pltpu.VMEM((MB, 128), f32),
             pltpu.VMEM((4, NY, MB + 8, 128), f32),
             pltpu.VMEM((4, NY, MB + 8, 128), f32),
             pltpu.VMEM((LAT * IMG, 2 * HD), bf16),
-            pltpu.VMEM((MB, 128), bf16),
             pltpu.VMEM((MB, 128), bf16),
             pltpu.VMEM((2, MB, 128), f32),
             pltpu.VMEM((2, MB, 128), f32),
@@ -486,17 +587,20 @@
             dma((4, NZ)), dma((4, NZ)),
             dma((2, NZ)), dma((2, NZ)),
             dma((2, 4)), dma((2, 4)),
+            dma((1,)), dma((1,)),
             dma((2, NZ)), dma((2, NZ)),
             dma((4, 4)), dma((4, 4)),
             dma((1,)), dma((1,)),
+            pltpu.SemaphoreType.REGULAR,
             dma((2, NZ)), dma((2, NZ)),
             dma((2, 4)), dma((2, 4)),
         ],
         compiler_params=pltpu.CompilerParams(
-            collective_id=0, has_side_effects=True, vmem_limit_bytes=48 * 2**20
+            collective_id=0, has_side_effects=True, vmem_limit_bytes=62 * 2**20
         ),
     )(
-        rows, picked, seen, norm_gain.astype(f32), wq[0], wkv[0], wo[0], alpha,
+        section_in[0], fresh, latents.reshape(72, VD), image_order, token_mask.transpose(0, 2, 1), norm_gain,
+        wq[0], wkv[0], wo[0], alpha,
     )
     out = out.transpose(0, 2, 1, 3, 4).reshape(2, 1, 2, D).astype(bf16)
     return out[0], out[1]

time: 179 us -> 139 us (0.78)
  the two profiles are of different devices: /device:TPU:6 before, /device:TPU:8 now
where the time goes in v2:
time: 139 us
  Pallas kernels  136 us (98%)
    pallas_call x1, Pallas kernels, local(): pl.pallas_call(kernel, out_shape=jax.ShapeDtypeStruct((2, NY, 2, NZ, 128)...  136 us

profile of v2, /device:TPU:8, one launch (start us, length us, event | category | flops | bytes accessed | tf_op | source)
XLA Modules:
  0.0 138.9 jit_solution(2806890389396140381)
XLA Ops:
  0.6 136.1 %shard_map.113 = f32[2,4,2,16,128]{4,3,2,1,0:T(8,128)} custom-call(bf16[2,8192]{1,0:T(2,128)(2,1)} %bitcast.17, bf16[2,8192]{1,0:T(2,128)(2,1)} %fresh_ref.1, bf16[72,1280]{1,0:T(8,128)(2,1)} %bitcast.15, s32[72]{0:T(128)} %order_ref.1, s32[9,8,128]{2,1,0:T(8,128)} %bitcast.16, bf16[1,8192]{1,0:T(2,128)(2,1)} %gain_ref.1, bf16[8192,128]{1,0:T(8,128)(2,1)} %bitcast.12, ...), custom_call_target="tpu_custom_call" | custom-call | tf_op jit(solution)/shard_map/pallas_call | solution.py:557
  136.7 0.9 convert_bitcast_fusion
  137.6 0.6 squeeze.23
  138.3 0.6 squeeze.22
  (3 shorter events, 0.0 us)

commit v3 on v2

--- a/solution.py
+++ b/solution.py
@@ -34,7 +34,7 @@
 
 
 TREE = both_ways([(6, 0), (2, 0), (1, 0), (3, 2), (4, 2), (8, 6), (7, 6), (5, 6)])
-LEAN = both_ways([(4, 0), (1, 0), (2, 1), (3, 4), (5, 4), (6, 5), (7, 6), (8, 7)])
+LEAN = both_ways([(3, 0), (1, 0), (6, 3), (4, 3), (2, 3), (7, 6), (5, 6), (8, 6)])
 STEPS = sorted({reached - via for tree in (TREE, LEAN) for reached, via in tree})
 
 
@@ -83,9 +83,9 @@
     section_ref, fresh_ref, latents_ref, order_ref, mask_ref, gain_ref, wq_ref, wkv_ref, wo_ref, alpha_ref,
     out_ref,
     wq_all, wo_all, wkv_all, rows32, entry, stripes, columns, first_blocks, blocks, lat_all, seen_all, gain32,
-    matrix, squares, partial, others, kv, relay_out, out_cols, out_rows, out_pairs,
+    matrix, squares, partial, others, kv, relay_out, out_cols, out_rows, out_pairs, gates, split_out, split_in, entered,
     local_sem, y_send, y_recv, w_send, w_recv, z_send, z_recv, l_send, l_recv, ly_send, ly_recv, lr_send, lr_recv,
-    c_send, c_recv, r_send, r_recv, n_send, n_recv, k_sem, oz_send, oz_recv, oy_send, oy_recv,
+    c_send, c_recv, r_send, r_recv, n_send, n_recv, k_sem, oz_send, oz_recv, oy_send, oy_recv, g_send, g_recv, h_send, h_recv,
 ):
     s = lax.axis_index("section")
     mp = lax.axis_index("mp")
@@ -181,6 +181,20 @@
                 )
             )
 
+    def swap_part(k, start, count):
+        for d in (2, 1, 3):
+            pending.append(
+                send(
+                    wo_ref.at[pl.ds(pl.multiple_of(lax.rem(y + d, NY) * QUARTER + start, 16), count)],
+                    wo_all.at[y, pl.ds(start, count)],
+                    w_send.at[k, d], w_recv.at[k, d], at_y(d),
+                )
+            )
+
+    def part_here(k, start, count):
+        for d in (1, 2, 3):
+            arrived(wo_all.at[lax.rem(y + NY - d, NY), pl.ds(start, count)], w_recv.at[k, d])
+
     def weights_here(k, dst):
         keeps[k].wait()
         for d in (1, 2, 3):
@@ -209,9 +223,14 @@
         for d in (1, 2, 3):
             arrived(lat_part(k, y), ly_send.at[k, d])
 
+    gates[y] = jnp.broadcast_to(jnp.tanh(alpha_ref[...]), (8, 128))
     swap_rows(0)
     swap_lat(0)
+    for d in (2, 1, 3):
+        pending.append(send(gates.at[y], gates.at[y], g_send.at[d], g_recv.at[d], at_y(d)))
+    swap_rows(1)
     swap_weights(0, wq_ref, wq_all)
+    swap_part(1, 0, 512)
     gain32[...] = gain_ref[...].astype(jnp.float32)
 
     row_at = lax.broadcasted_iota(jnp.int32, (MB, MB), 0)
@@ -255,13 +274,12 @@
     gathers[0].pass_on(0)
     lat_swapped(0)
     lat_gathers[0].pass_on(0)
-    swap_rows(1)
     gathers[0].pass_on(2, 6)
-    lat_gathers[0].pass_on(1, 4)
+    lat_gathers[0].pass_on(3)
     rows_here(1)
     gathers[0].finish()
     signal(k_sem, previous)
-    lat_gathers[0].pass_on(5)
+    lat_gathers[0].pass_on(6)
 
     def column_rows(which):
         return pl.ds(pl.multiple_of(which * 8, 8), 8)
@@ -377,7 +395,9 @@
 
     def start_out(k, made):
         out_cols[k] = made.astype(jnp.float32)
-
+        send_out(k)
+
+    def send_out(k):
         @pl.loop(1, NZ)
         def _(d):
             send(
@@ -387,11 +407,13 @@
 
         out_rows[k, column_rows(z), :] = out_cols[k, column_rows(z), :]
 
-    def turn_out(k):
+    def out_arrived(k):
         @pl.loop(1, NZ)
         def _(d):
             arrived(out_rows.at[k, column_rows(lax.rem(z + NZ - d, NZ))], oz_recv.at[k, d])
 
+    def turn_out(k):
+        out_arrived(k)
         for target in range(NY):
             for token in range(2):
                 out_pairs[k, target, token] = out_rows[k, pl.ds(2 * target + token, NZ, stride=8), :]
@@ -414,24 +436,23 @@
             ref = out_cols.at[k, column_rows(lax.rem(z + d, NZ))]
             pltpu.make_async_copy(ref, ref, oz_send.at[k, d]).wait()
 
+    start_columns(0)
+    start_columns(1)
     matrix_of_rows()
     weights_here(0, wq_all)
     start_sums(0, wq_all, True)
-    swap_weights(1, wo_ref, wo_all)
-    lat_gathers[0].pass_on(6, 7)
     keeps[2].wait()
     keeps[3].wait()
     lat_gathers[0].finish()
     make_kv(0)
-    blocks[0, z] = attend(0, sums(0, True))
+    query_sums = sums(0, True)
+    swap_part(2, 512, QUARTER - 512)
+    blocks[0, z] = attend(0, query_sums)
     gathers[1].pass_on(0)
 
     @pl.when(s < 7)
     def _():
         send(lat_all.at[0], lat_all.at[1], lr_send.at[0], lr_recv.at[0], following)
-
-    start_columns(0)
-    start_columns(1)
 
     @pl.when(s == 0)
     def _():
@@ -447,7 +468,9 @@
         lat_gathers[1].pass_on(2, 6)
 
     matrix_plain(1)
-    weights_here(1, wo_all)
+    keeps[1].wait()
+    part_here(1, 0, 512)
+    part_here(2, 512, QUARTER - 512)
     start_sums(1, wo_all, False)
     pl.semaphore_wait(k_sem, 1)
 
@@ -514,13 +537,60 @@
 
     gathers[3].pass_on(0)
     gathers[3].pass_on(2, 6)
+    out_here(0)
+
+    @pl.when(s < 7)
+    def _():
+        send(out_ref.at[0], entered, h_send.at[0], h_recv.at[0], following)
+
     gathers[3].finish()
     matrix_plain(3)
-    start_sums(3, wo_all, False)
-    start_out(1, block_out(sums(3, False), blocks[1, z].astype(jnp.float32)))
-    turn_out(1)
-    out_here(0)
-    out_here(1)
+    for part in range(NY):
+        partial[3, part, pl.ds(0, MB), :] = jnp.dot(
+            matrix[...], wo_all[part], preferred_element_type=jnp.float32
+        )
+        for owner in range(NY):
+            for token in range(2):
+                split_out[owner, pl.ds(part * 32 + token * NZ, NZ), :] = partial[
+                    3, part, pl.ds(2 * owner + token, NZ, stride=8), :
+                ]
+    for d in (2, 1, 3):
+        pending.append(
+            send(
+                split_out.at[lax.rem(y + d, NY)], others.at[3, y, pl.ds(0, MB)],
+                r_send.at[3, d], r_recv.at[3, d], at_y(d),
+            )
+        )
+    for d in (1, 2, 3):
+        arrived(gates.at[lax.rem(y + NY - d, NY)], g_recv.at[d])
+        arrived(others.at[3, lax.rem(y + NY - d, NY), pl.ds(0, MB)], r_recv.at[3, d])
+    total = split_out[y]
+    for d in (1, 2, 3):
+        total = total + others[3, lax.rem(y + NY - d, NY), pl.ds(0, MB), :]
+    for part in range(NY):
+        rows = slice(part * 32, part * 32 + 32)
+        split_in[rows, :] = (total[rows] * gates[part, 0:1, :]).astype(jnp.bfloat16).astype(jnp.float32)
+    for owner in range(NZ):
+        out_cols[1, pl.ds(owner * 8, 8), :] = split_in[pl.ds(owner, 8, stride=NZ), :]
+    send_out(1)
+
+    @pl.when(s > 0)
+    def _():
+        arrived(entered, h_recv.at[0])
+
+    @pl.when(s == 0)
+    def _():
+        for part in range(NY):
+            for token in range(2):
+                for at in range(NZ):
+                    lane = (part * NZ + at) * 128
+                    entered[part, token, pl.ds(at, 1), :] = rows32[1, pl.ds(token, 1), pl.ds(lane, 128)]
+
+    out_arrived(1)
+    for part in range(NY):
+        for token in range(2):
+            branch = out_rows[1, pl.ds(2 * part + token, NZ, stride=8), :]
+            out_ref[1, part, token] = entered[part, token] + branch
 
     gathers[0].drain()
     gathers[1].drain()
@@ -539,6 +609,7 @@
         for hop in hops:
             arrived(relay_out, z_send.at[2, hop % NZ])
         arrived(relay_out, n_send.at[0])
+        arrived(out_ref.at[0], h_send.at[0])
         arrived(lat_all.at[0], lr_send.at[0])
 
     for copy in pending:
@@ -581,9 +652,13 @@
             pltpu.VMEM((2, MB, 128), f32),
             pltpu.VMEM((2, MB, 128), f32),
             pltpu.VMEM((2, NY, 2, NZ, 128), f32),
+            pltpu.VMEM((NY, 8, 128), f32),
+            pltpu.VMEM((NY, MB, 128), f32),
+            pltpu.VMEM((MB, 128), f32),
+            pltpu.VMEM((NY, 2, NZ, 128), f32),
             dma((4,)),
             dma((2, 4)), dma((2, 4)),
-            dma((2, 4)), dma((2, 4)),
+            dma((3, 4)), dma((3, 4)),
             dma((4, NZ)), dma((4, NZ)),
             dma((2, NZ)), dma((2, NZ)),
             dma((2, 4)), dma((2, 4)),
@@ -594,6 +669,8 @@
             pltpu.SemaphoreType.REGULAR,
             dma((2, NZ)), dma((2, NZ)),
             dma((2, 4)), dma((2, 4)),
+            dma((4,)), dma((4,)),
+            dma((1,)), dma((1,)),
         ],
         compiler_params=pltpu.CompilerParams(
             collective_id=0, has_side_effects=True, vmem_limit_bytes=62 * 2**20

time: 139 us -> 136 us (0.978)
  the two profiles are of different devices: /device:TPU:8 before, /device:TPU:6 now
where the time goes in v3:
time: 136 us; the launch traced here: 134 us
  Pallas kernels  131 us (96%)
    pallas_call x1, Pallas kernels, local(): pl.pallas_call(kernel, out_shape=jax.ShapeDtypeStruct((2, NY, 2, NZ, 128)...  131 us

profile of v3, /device:TPU:6, one launch (start us, length us, event | category | flops | bytes accessed | tf_op | source)
XLA Modules:
  0.0 133.9 jit_solution(1381301333303095648)
XLA Ops:
  0.6 131.1 %shard_map.113 = f32[2,4,2,16,128]{4,3,2,1,0:T(8,128)} custom-call(bf16[2,8192]{1,0:T(2,128)(2,1)} %bitcast.17, bf16[2,8192]{1,0:T(2,128)(2,1)} %fresh_ref.1, bf16[72,1280]{1,0:T(8,128)(2,1)} %bitcast.15, s32[72]{0:T(128)} %order_ref.1, s32[9,8,128]{2,1,0:T(8,128)} %bitcast.16, bf16[1,8192]{1,0:T(2,128)(2,1)} %gain_ref.1, bf16[8192,128]{1,0:T(8,128)(2,1)} %bitcast.12, ...), custom_call_target="tpu_custom_call" | custom-call | tf_op jit(solution)/shard_map/pallas_call | solution.py:628
  131.7 0.9 convert_bitcast_fusion
  132.7 0.6 squeeze.23
  133.3 0.6 squeeze.22
  (3 shorter events, 0.0 us)

commit v4 on v3

--- a/solution.py
+++ b/solution.py
@@ -230,7 +230,7 @@
         pending.append(send(gates.at[y], gates.at[y], g_send.at[d], g_recv.at[d], at_y(d)))
     swap_rows(1)
     swap_weights(0, wq_ref, wq_all)
-    swap_part(1, 0, 512)
+    swap_part(1, 0, 1024)
     gain32[...] = gain_ref[...].astype(jnp.float32)
 
     row_at = lax.broadcasted_iota(jnp.int32, (MB, MB), 0)
@@ -446,7 +446,7 @@
     lat_gathers[0].finish()
     make_kv(0)
     query_sums = sums(0, True)
-    swap_part(2, 512, QUARTER - 512)
+    swap_part(2, 1024, QUARTER - 1024)
     blocks[0, z] = attend(0, query_sums)
     gathers[1].pass_on(0)
 
@@ -469,8 +469,8 @@
 
     matrix_plain(1)
     keeps[1].wait()
-    part_here(1, 0, 512)
-    part_here(2, 512, QUARTER - 512)
+    part_here(1, 0, 1024)
+    part_here(2, 1024, QUARTER - 1024)
     start_sums(1, wo_all, False)
     pl.semaphore_wait(k_sem, 1)
 

time: 136 us -> 134 us (0.985)
  the two profiles are of different devices: /device:TPU:6 before, /device:TPU:2 now
where the time goes in v4:
time: 134 us
  Pallas kernels  131 us (98%)
    pallas_call x1, Pallas kernels, local(): pl.pallas_call(kernel, out_shape=jax.ShapeDtypeStruct((2, NY, 2, NZ, 128)...  131 us

profile of v4, /device:TPU:2, one launch (start us, length us, event | category | flops | bytes accessed | tf_op | source)
XLA Modules:
  0.0 133.8 jit_solution(4922427041178117467)
XLA Ops:
  0.6 131.0 %shard_map.113 = f32[2,4,2,16,128]{4,3,2,1,0:T(8,128)} custom-call(bf16[2,8192]{1,0:T(2,128)(2,1)} %bitcast.17, bf16[2,8192]{1,0:T(2,128)(2,1)} %fresh_ref.1, bf16[72,1280]{1,0:T(8,128)(2,1)} %bitcast.15, s32[72]{0:T(128)} %order_ref.1, s32[9,8,128]{2,1,0:T(8,128)} %bitcast.16, bf16[1,8192]{1,0:T(2,128)(2,1)} %gain_ref.1, bf16[8192,128]{1,0:T(8,128)(2,1)} %bitcast.12, ...), custom_call_target="tpu_custom_call" | custom-call | tf_op jit(solution)/shard_map/pallas_call | solution.py:628
  131.6 0.9 convert_bitcast_fusion
  132.6 0.6 squeeze.23
  133.2 0.6 squeeze.22
  (3 shorter events, 0.0 us)
